TPU v7x, 128 devices: a whole 4x4x4 slice. The times are simulated.
128 devices in a mesh: ctx: 16 (over y, z_hi, core), fsdp: 8 (over x, z_lo).
Axes of the slice: x: 4, y: 4, z: 4 (z_hi: 2, z_lo: 2; z = z_hi * 2 + z_lo), core: 2. Of those that a mesh axis runs over, the one named last changes fastest.
Arguments:
- tokens: bfloat16 [8, 2048, 7168], P('fsdp', 'ctx'), may hold values from -16 to 16
- kv_weight: bfloat16 [7168, 576], P('fsdp'), may hold values from -0.0625 to 0.0625
- latent_gain: float32 [512], replicated, may hold values from 0.1 to 1.9
- queries: bfloat16 [8, 2048, 32, 576], P('fsdp', 'ctx'), may hold values from -40 to 40
- out_grad: bfloat16 [8, 2048, 32, 512], P('fsdp', 'ctx'), may hold values from -6 to 6
- segment_ids: int32 [8, 2048], P('fsdp', 'ctx'), may hold values from 0 to 7, never falling along the last dimension, each value on 1 to 1024 neighbouring positions
Outputs:
- attended: bfloat16 [8, 2048, 32, 512], P('fsdp', 'ctx')
- logit_max: float32 [32], replicated
- update: float32 [7168, 576], P(('ctx', 'fsdp'))
Inputs may be any that keep to these rules, and one draw needn't show every extreme that they name: `segment_ids`: within each rollout the document numbers never fall; each document holds 1 to 1024 positions, and one holds exactly 1024.
All inputs are finite; a program needn't handle non-finite values.
Results may differ from a plain program's by a relative error of at most 0.022.
Values may be sent and summed in bfloat16 or wider, within the bound.
A program may use at most 320 MiB of HBM per device.

v0:
```python
import functools
import math

import jax
import jax.numpy as jnp
from jax import lax
from jax.experimental import pallas as pl
from jax.experimental.pallas import tpu as pltpu
from jax.sharding import PartitionSpec as P

D = 7168
LAT = 512
ROPE = 64
HEADS = 32
NS_ITERS = 5
KV = LAT + ROPE
PAD = 640
HALF = ROPE // 2
BLOCK = 128
REACH = 8
SLOTS = REACH + 1
WINDOW = SLOTS * BLOCK
CTX = 16
FSDP = 8
SHARD = D // FSDP
PIECE = SHARD // CTX
TILE_Q = 16
ROWS = TILE_Q * HEADS
TILES = BLOCK // TILE_Q

attn_scale = 192.0 ** (-0.5)
rope_base = 50000.0
quintic_a = 3.4445
quintic_b = -4.775
quintic_c = 2.0315
BIG = -1e30
MiB = 1 << 20

MESH = pl.DeviceIdType.MESH
VMEM = pl.BlockSpec(memory_space=pltpu.VMEM)
ANY = pl.BlockSpec(memory_space=pl.ANY)
f32, bf16 = jnp.float32, jnp.bfloat16


def rope_tables(positions):
    ladder = jnp.arange(HALF, dtype=f32)
    freqs = jnp.power(rope_base, -2.0 * ladder / ROPE)
    angles = positions.astype(f32)[:, None] * freqs[None, :]
    return (jnp.cos(angles), jnp.sin(angles))


def nn(a, b, **kw):
    return lax.dot_general(a, b, (((1,), (0,)), ((), ())), preferred_element_type=f32, **kw)


def nt(a, b, **kw):
    return lax.dot_general(a, b, (((1,), (1,)), ((), ())), preferred_element_type=f32, **kw)


def tn(a, b, **kw):
    return lax.dot_general(a, b, (((0,), (0,)), ((), ())), preferred_element_type=f32, **kw)


class Place:
    def __init__(self):
        self.c, self.f = lax.axis_index("ctx"), lax.axis_index("fsdp")
        self.y, self.zh, self.k = self.c // 4, (self.c // 2) % 2, self.c % 2
        self.x, self.zl = self.f // 2, self.f % 2

    def at(self, x=None, y=None, zh=None, zl=None, k=None):
        x = self.x if x is None else x
        y = self.y if y is None else y
        zh = self.zh if zh is None else zh
        zl = self.zl if zl is None else zl
        k = self.k if k is None else k
        return ((y * 2 + zh) * 2 + k, x * 2 + zl)

    def ctx(self, c):
        return (c, self.f)

    def fsdp(self, f):
        return (self.c, f)


def greet(devices, others=0):
    barrier = pltpu.get_barrier_semaphore()
    for device in devices:
        pl.semaphore_signal(barrier, inc=1, device_id=device, device_id_type=MESH)
    pl.semaphore_wait(barrier, len(devices) + others)


def send(src, dst, send_sem, recv_sem, device):
    return pltpu.make_async_remote_copy(
        src_ref=src,
        dst_ref=dst,
        send_sem=send_sem,
        recv_sem=recv_sem,
        device_id=device,
        device_id_type=MESH,
    )


def keys_kernel(
    tok_hbm, w, gain, hot, cos, sin, qt, keys_out, proj_out, q_out, wall, win, tok, qin, qrow, qs, ws, wr, ks, kr
):
    me = Place()
    c, k, x = me.c, me.k, me.x
    sibling = me.at(k=1 - k)
    z_same, z_other = me.at(zl=1 - me.zl), me.at(zl=1 - me.zl, zh=1 - me.zh)
    x_up, x_down = me.at(x=(x + 1) % 4), me.at(x=(x + 3) % 4)
    later = [me.ctx((c + 2 * j) % CTX) for j in range(1, 5)]
    earlier = [me.ctx((c - 2 * j + CTX) % CTX) for j in range(1, 5)]
    greet([sibling, z_same, z_other, x_up, x_down] + later + earlier[:3])

    half = KV // 2
    quarter = half // 2
    counter = [0]

    def rows(core, q=None):
        if q is None:
            return pl.ds(pl.multiple_of(core * half, 16), half)
        return pl.ds(pl.multiple_of(core * half + q * quarter, 16), quarter)

    def post(src_f, src, core, q, device):
        i = counter[0]
        counter[0] += 1
        where = rows(core, q)
        source = w.at[where] if src is None else src.at[src_f, where]
        copy = send(source, wall.at[src_f, where], ws.at[i], wr.at[i], device)
        copy.start()
        return copy

    def shard_of(xx, zl):
        return (xx % 4) * 2 + zl

    own = me.f
    up = [post(own, None, k, 0, x_up), post(own, None, k, 1, x_up)]
    down = [post(own, None, k, 1, x_down), post(own, None, k, 0, x_down)]
    own_z = [post(own, None, k, 0, z_same), post(own, None, k, 1, z_other)]
    fetch = pltpu.make_async_copy(qt, qin, qs.at[0])
    fetch.start()
    fetch_w = pltpu.make_async_copy(w, wall.at[own], qs.at[1])
    fetch_w.start()
    fetch_tok = pltpu.make_async_copy(tok_hbm, tok, qs.at[2])
    fetch_tok.start()
    posted = up + down + own_z

    def forward(copy, shard, q):
        copy.wait_recv()
        z = post(shard, wall, k, q, (z_same, z_other)[q])
        s = post(shard, wall, k, q, sibling)
        posted.extend([z, s])
        return z, s

    def pass_on(copy, shard, q):
        copy.wait_recv()
        s = post(shard, wall, k, q, sibling)
        posted.append(s)
        return s

    other = 1 - me.zl
    f_prev, f_next, f_far = shard_of(x + 3, me.zl), shard_of(x + 1, me.zl), shard_of(x + 2, me.zl)
    o_own, o_prev, o_next, o_far = (shard_of(x + i, other) for i in (0, 3, 1, 2))

    def add(total, shard):
        return total + nt(
            tok[:, pl.ds(pl.multiple_of(shard * SHARD, 128), SHARD)], wall[shard]
        )

    fetch.wait()

    def turn(h, _):
        for lanes in range(PAD // 128):
            width = min(128, KV - lanes * 128)
            block = qin[h, lanes * 128 : lanes * 128 + width, :].astype(f32)
            if width < 128:
                block = jnp.concatenate([block, jnp.zeros((128 - width, BLOCK), f32)], axis=0)
            qrow[lanes, pl.ds(h, BLOCK, stride=HEADS), :] = block.T
        return 0

    lax.fori_loop(0, HEADS // 2, turn, 0)

    prev0 = forward(up[0], f_prev, 0)
    relay_up = post(f_prev, wall, k, 0, x_up)
    next1 = forward(down[0], f_next, 1)
    relay_down = post(f_next, wall, k, 1, x_down)
    posted.extend([relay_up, relay_down])
    s_own = [pass_on(own_z[q], o_own, q) for q in range(2)]
    lax.fori_loop(HEADS // 2, HEADS, turn, 0)
    fetch_w.wait()
    fetch_tok.wait()
    acc = nt(tok[:, pl.ds(pl.multiple_of(own * SHARD, 128), SHARD)], wall[own])
    prev1 = forward(up[1], f_prev, 1)
    next0 = forward(down[1], f_next, 0)
    s_prev0 = pass_on(prev0[0], o_prev, 0)
    s_next1 = pass_on(next1[0], o_next, 1)

    def narrow(i, _):
        rows = pl.ds(pl.multiple_of(i * ROWS, ROWS), ROWS)
        for lanes in range(PAD // 128):
            width = min(128, KV - lanes * 128)
            q_out[rows, lanes * 128 : lanes * 128 + width] = qrow[lanes, rows, :width].astype(bf16)
        return 0

    lax.fori_loop(0, TILES, narrow, 0)
    for copy in s_own:
        copy.wait_recv()
    acc = add(acc, o_own)
    far0 = forward(relay_up, f_far, 0)
    far1 = forward(relay_down, f_far, 1)
    prev0[1].wait_recv()
    prev1[1].wait_recv()
    acc = add(acc, f_prev)
    next0[1].wait_recv()
    next1[1].wait_recv()
    acc = add(acc, f_next)
    s_prev1 = pass_on(prev1[0], o_prev, 1)
    s_next0 = pass_on(next0[0], o_next, 0)
    far0[1].wait_recv()
    far1[1].wait_recv()
    acc = add(acc, f_far)
    s_far0 = pass_on(far0[0], o_far, 0)
    s_far1 = pass_on(far1[0], o_far, 1)
    for shard, pair in ((o_prev, (s_prev0, s_prev1)), (o_next, (s_next0, s_next1)), (o_far, (s_far0, s_far1))):
        for copy in pair:
            copy.wait_recv()
        acc = add(acc, shard)

    compressed = acc[:, :LAT]
    inverse = lax.rsqrt(jnp.mean(compressed * compressed, axis=1, keepdims=True) + 1e-06)
    latent = compressed * inverse * gain[...]
    first, second = acc[:, LAT : LAT + HALF], acc[:, LAT + HALF :]
    mine = win.at[SLOTS - 1]
    mine[:, :LAT] = latent.astype(bf16)
    tail = jnp.concatenate(
        [
            first * cos[...] - second * sin[...],
            second * cos[...] + first * sin[...],
            hot[...],
        ],
        axis=1,
    )
    mine[:, LAT:] = tail.astype(bf16)
    proj_out[...] = acc

    def slot(distance):
        return SLOTS - 1 - distance

    spread = []
    for j in range(1, 5):
        copy = send(mine, win.at[slot(2 * j)], ks.at[j - 1], kr.at[j - 1], later[j - 1])
        copy.start()
        spread.append(copy)
    to_sibling = []

    def give(n):
        copy = send(
            win.at[slot(2 * n + 2 * k)], win.at[slot(2 * n + 1)], ks.at[4 + n], kr.at[4 + n], sibling
        )
        copy.start()
        to_sibling.append(copy)

    spread[0].wait_recv()
    give(0)
    give_next = 1
    for j in range(1, 4):
        spread[j].wait_recv()
        give(give_next)
        give_next += 1
    for copy in to_sibling:
        copy.wait_recv()
    lane = lax.broadcasted_iota(jnp.int32, (BLOCK, 128), 1)
    flag = jnp.where(lane == ROPE + 8, 1.0, 0.0)
    for d in range(REACH + 1):
        keys_out[slot(d)] = win[slot(d)]
        if d > 0:

            @pl.when(c < d)
            def _(d=d):
                keys_out[slot(d), :, LAT:] = flag.astype(bf16)

    for copy in posted + spread + to_sibling:
        copy.wait_send()


N_W = 6 + 2 + 6 * 2 + 8


def make_keys(tok, w, gain, hot, cos, sin, qt):
    return pl.pallas_call(
        keys_kernel,
        out_shape=(
            jax.ShapeDtypeStruct((SLOTS, BLOCK, PAD), bf16),
            jax.ShapeDtypeStruct((BLOCK, KV), f32),
            jax.ShapeDtypeStruct((BLOCK * HEADS, KV), bf16),
        ),
        in_specs=[ANY, ANY] + [VMEM] * 4 + [ANY],
        out_specs=(VMEM,) * 3,
        scratch_shapes=[
            pltpu.VMEM((FSDP, KV, SHARD), bf16),
            pltpu.VMEM((SLOTS, BLOCK, PAD), bf16),
            pltpu.VMEM((BLOCK, D), bf16),
            pltpu.VMEM((HEADS, KV, BLOCK), bf16),
            pltpu.VMEM((PAD // 128, BLOCK * HEADS, 128), f32),
            pltpu.SemaphoreType.DMA((3,)),
            pltpu.SemaphoreType.DMA((N_W,)),
            pltpu.SemaphoreType.DMA((N_W,)),
            pltpu.SemaphoreType.DMA((8,)),
            pltpu.SemaphoreType.DMA((8,)),
        ],
        compiler_params=pltpu.CompilerParams(
            collective_id=0, has_side_effects=True, vmem_limit_bytes=48 * MiB
        ),
        name="keys",
    )(tok, w, gain, hot, cos, sin, qt)


def attention_kernel(
    q, dout, hot, keys, att_out, grad_out, peak_out, vt, qr, s_scr, d_scr, p_scr
):
    t = pl.program_id(0)

    @pl.when(t == 0)
    def _():
        grad_out[...] = jnp.zeros_like(grad_out)
        peak_out[...] = jnp.full_like(peak_out, BIG)
        for j in range(SLOTS):
            vt[:, j * BLOCK : (j + 1) * BLOCK] = keys[j * BLOCK : (j + 1) * BLOCK, :LAT].T

    qr[:, :ROPE] = q[:, LAT:]
    lane = lax.broadcasted_iota(jnp.int32, (TILE_Q, ROPE), 1)
    qmask = jnp.where((lane < 9) & (hot[...] == 0.0), BIG, 0.0)
    spread = jnp.broadcast_to(qmask[:, None, :], (TILE_Q, HEADS, ROPE))
    qr[:, ROPE:] = spread.reshape(ROWS, ROPE).astype(bf16)

    own = slice(WINDOW - BLOCK, WINDOW)
    s_scr[...] = nt(keys[:, :LAT], q[:, :LAT]) + nt(keys[:, LAT:], qr[...])
    d_scr[...] = nt(keys[:, :LAT], dout[...])
    key = lax.broadcasted_iota(jnp.int32, (BLOCK, ROWS), 0)
    query = t * TILE_Q + lax.broadcasted_iota(jnp.int32, (BLOCK, ROWS), 1) // HEADS
    s_scr[own, :] = jnp.where(key <= query, s_scr[own, :], BIG)
    peak = jnp.max(s_scr[...], axis=0, keepdims=True)
    peak_out[...] = jnp.maximum(peak_out[...], peak * attn_scale)
    total = jnp.zeros((1, ROWS), f32)
    for j in range(SLOTS):
        at = slice(j * BLOCK, (j + 1) * BLOCK)
        e = jnp.exp((s_scr[at, :] - peak) * attn_scale)
        s_scr[at, :] = e
        total = total + jnp.sum(e, axis=0, keepdims=True)
    share = 1.0 / total
    for j in range(SLOTS):
        at = slice(j * BLOCK, (j + 1) * BLOCK)
        p_scr[at, :] = (s_scr[at, :] * share).astype(bf16)
    attended = nn(vt[...], p_scr[...]).T.astype(bf16)
    grad_out[:, :LAT] += nn(p_scr[...], dout[...])
    att_out[...] = attended
    delta = jnp.sum(dout[...].astype(f32) * attended.astype(f32), axis=1, keepdims=True)
    delta = jnp.broadcast_to(delta, (ROWS, 128)).T[:1, :]
    share = share * attn_scale
    for j in range(SLOTS):
        at = slice(j * BLOCK, (j + 1) * BLOCK)
        p_scr[at, :] = (s_scr[at, :] * share * (d_scr[at, :] - delta)).astype(bf16)
    grad_out[...] += nn(p_scr[...], q[...])


def attention(q, dout, hot, keys):
    per_tile = lambda width: pl.BlockSpec((ROWS, width), lambda t: (t, 0))
    whole = lambda *shape: pl.BlockSpec(shape, lambda t: (0, 0))
    flops = 2 * BLOCK * HEADS * WINDOW // 2 * (2 * KV + 3 * LAT)
    return pl.pallas_call(
        attention_kernel,
        grid=(TILES,),
        in_specs=[
            per_tile(KV),
            per_tile(LAT),
            pl.BlockSpec((TILE_Q, ROPE), lambda t: (t, 0)),
            whole(WINDOW, PAD),
        ],
        out_specs=[per_tile(LAT), whole(WINDOW, KV), whole(8, ROWS)],
        scratch_shapes=[
            pltpu.VMEM((LAT, WINDOW), bf16),
            pltpu.VMEM((ROWS, 128), bf16),
            pltpu.VMEM((WINDOW, ROWS), f32),
            pltpu.VMEM((WINDOW, ROWS), f32),
            pltpu.VMEM((WINDOW, ROWS), bf16),
        ],
        out_shape=(
            jax.ShapeDtypeStruct((BLOCK * HEADS, LAT), bf16),
            jax.ShapeDtypeStruct((WINDOW, KV), f32),
            jax.ShapeDtypeStruct((8, ROWS), f32),
        ),
        compiler_params=pltpu.CompilerParams(
            dimension_semantics=("arbitrary",), vmem_limit_bytes=32 * MiB
        ),
        cost_estimate=pl.CostEstimate(
            flops=flops, bytes_accessed=16 << 20, transcendentals=BLOCK * HEADS * WINDOW
        ),
        name="attention",
    )(q, dout, hot, keys)


def grads_kernel(
    kg, proj, gain, cos, sin, tok, peak, rows_out, peak_out,
    near, outbox, far, kvg, peaks, tok_in, tok_t, part, part_in, sums, sums_in,
    ns, nr, fs, fr, gs, gr, ps, pr, ss, sr, ts, tr, as_, ar,
):
    me = Place()
    c, k, f = me.c, me.k, me.f
    sibling = me.at(k=1 - k)
    back = [me.ctx((c - 2 * j + CTX) % CTX) for j in range(1, 8)]
    peers = [me.fsdp((f + s) % FSDP) for s in range(1, FSDP)]
    greet([sibling] + back + peers)

    def slot(distance):
        return SLOTS - 1 - distance

    swaps = []
    for n in range(4):
        copy = send(kg.at[slot(2 * n + 1)], near.at[n], ns.at[n], nr.at[n], sibling)
        copy.start()
        swaps.append(copy)
    tokens = []
    for s in range(1, FSDP):
        columns = pl.ds(pl.multiple_of(((f + s) % FSDP) * SHARD, 128), SHARD)
        copy = send(tok.at[:, columns], tok_in.at[s], as_.at[s - 1], ar.at[s - 1], peers[s - 1])
        copy.start()
        tokens.append(copy)
    gathers = []
    for s in range(1, FSDP):
        copy = send(peak, peaks.at[s], ps.at[s - 1], pr.at[s - 1], peers[s - 1])
        copy.start()
        gathers.append(copy)
    sends = []
    own = kg[slot(0)]
    for copy in swaps:
        copy.wait_recv()

    @pl.when(k == 1)
    def _():
        for n in range(4):
            outbox[n] = near[n] + kg[slot(2 * n + 2)]

    @pl.when(k == 0)
    def _():
        for n in range(3):
            outbox[n] = near[n + 1] + kg[slot(2 * n + 2)]
        outbox[3] = kg[slot(8)]

    own = own + jnp.where(k == 0, near[0], jnp.zeros_like(own))
    for n in range(4):
        copy = send(outbox.at[n], far.at[n], fs.at[n], fr.at[n], back[n])
        copy.start()
        sends.append(copy)
    tok_t[:, :BLOCK] = tok[:, pl.ds(pl.multiple_of(f * SHARD, 128), SHARD)].T
    for s in range(1, FSDP):
        tokens[s - 1].wait_recv()
        tok_t[:, s * BLOCK : (s + 1) * BLOCK] = tok_in[s].T
    for copy in sends:
        copy.wait_recv()
    key_grad = own
    for n in range(4):
        key_grad = key_grad + far[n]

    compressed = proj[:, :LAT]
    inverse = lax.rsqrt(jnp.mean(compressed * compressed, axis=1, keepdims=True) + 1e-06)
    first, second = key_grad[:, LAT : LAT + HALF], key_grad[:, LAT + HALF :]
    d_first = first * cos[...] + second * sin[...]
    d_second = -first * sin[...] + second * cos[...]
    scaled = key_grad[:, :LAT] * gain[...]
    inner = jnp.mean(compressed * scaled, axis=1, keepdims=True)
    d_comp = inverse * (scaled - compressed * (inverse * inverse * inner))
    kvg[0, :, :LAT] = d_comp.astype(bf16)
    kvg[0, :, LAT:] = jnp.concatenate([d_first, d_second], axis=1).astype(bf16)
    spread = []
    for s in range(1, FSDP):
        copy = send(kvg.at[0], kvg.at[s], gs.at[s - 1], gr.at[s - 1], peers[s - 1])
        copy.start()
        spread.append(copy)
    top = peak[...]
    for s in range(1, FSDP):
        gathers[s - 1].wait_recv()
        top = jnp.maximum(top, peaks[s])
    for copy in spread:
        copy.wait_recv()

    everything = kvg[...].reshape(FSDP * BLOCK, KV)

    def multiply(n, core):
        p = 2 * n + core
        rows = pl.ds(pl.multiple_of(p * PIECE, 8), PIECE)
        return nn(tok_t[rows, :], everything)

    whole = nn(tok_t[...], everything)
    for p in range(CTX):
        part[p, :, :KV] = whole[p * PIECE : (p + 1) * PIECE]
        for r in range(8):
            part[p, r : r + 1, KV:] = top[r : r + 1, r * ROPE : (r + 1) * ROPE]
    halves = []
    for n in range(CTX // 2):
        copy = send(part.at[2 * n + 1 - k], part_in.at[n], ss.at[n], sr.at[n], sibling)
        copy.start()
        halves.append(copy)
    totals = []
    me_n = c // 2
    for n in range(CTX // 2):
        halves[n].wait_recv()
        here = part.at[2 * n + k]
        sums[n, :, :KV] = here[:, :KV] + part_in[n, :, :KV]
        sums[n, :8, KV:] = jnp.maximum(here[:8, KV:], part_in[n, :8, KV:])
    for s in range(1, CTX // 2):
        to = (me_n - s + 8) % 8
        copy = send(sums.at[to], sums_in.at[s], ts.at[s], tr.at[s], back[s - 1])
        copy.start()
        totals.append(copy)
    rows = sums[me_n, :, :KV]
    top = sums[me_n, :8, KV:]
    for s in range(1, CTX // 2):
        totals[s - 1].wait_recv()
        rows = rows + sums_in[s, :, :KV]
        top = jnp.maximum(top, sums_in[s, :8, KV:])
    rows_out[...] = rows
    peak_out[...] = top
    for copy in swaps + tokens + gathers + sends + spread + halves + totals:
        copy.wait_send()


def weight_grad(kg, proj, gain, cos, sin, tok, peak):
    sems = [4, 4, 4, 4, 7, 7, 7, 7, 8, 8, 8, 8, 7, 7]
    return pl.pallas_call(
        grads_kernel,
        out_shape=(
            jax.ShapeDtypeStruct((PIECE, KV), f32),
            jax.ShapeDtypeStruct((8, ROPE), f32),
        ),
        in_specs=[VMEM] * 7,
        out_specs=(VMEM, VMEM),
        scratch_shapes=[
            pltpu.VMEM((4, BLOCK, KV), f32),
            pltpu.VMEM((4, BLOCK, KV), f32),
            pltpu.VMEM((4, BLOCK, KV), f32),
            pltpu.VMEM((FSDP, BLOCK, KV), bf16),
            pltpu.VMEM((FSDP, 8, ROWS), f32),
            pltpu.VMEM((FSDP, BLOCK, SHARD), bf16),
            pltpu.VMEM((SHARD, FSDP * BLOCK), bf16),
            pltpu.VMEM((CTX, PIECE, PAD), f32),
            pltpu.VMEM((CTX // 2, PIECE, PAD), f32),
            pltpu.VMEM((CTX // 2, PIECE, PAD), f32),
            pltpu.VMEM((CTX // 2, PIECE, PAD), f32),
        ]
        + [pltpu.SemaphoreType.DMA((n,)) for n in sems],
        compiler_params=pltpu.CompilerParams(
            collective_id=1, has_side_effects=True, vmem_limit_bytes=32 * MiB
        ),
        name="weight_grad",
    )(kg, proj, gain, cos, sin, tok, peak)


TRI = [(r, s) for r in range(5) for s in range(r, 5)]
PACKED = 2048
PAIRS = {3: [(0, 0), (0, 1), (1, 0)], 6: [(0, 0), (0, 1), (1, 0), (0, 2), (2, 0), (1, 1)]}


def split(value, count):
    parts = []
    for _ in range(count):
        part = value.astype(bf16)
        parts.append(part)
        value = value - part.astype(f32)
    return parts


def muon_kernel(
    g, out, pack, core_in, yz_in, x_in, acc, gram, rows_in, a_scr, left_scr, thin_scr, right_scr, ms, mr, cs, cr, ys, yr, xs, xr, xs2, xr2, ys2, yr2, cs2, cr2
):
    me = Place()
    k, x, y = me.k, me.x, me.y
    z = me.zh * 2 + me.zl
    sibling = me.at(k=1 - k)

    def plane(n):
        yy, zz = (y + n // 4) % 4, (z + n % 4) % 4
        return me.at(y=yy, zh=zz // 2, zl=zz % 2), yy * 4 + zz

    planes = [plane(n) for n in range(16)]
    line = [me.at(x=(x + s) % 4) for s in range(4)]
    give = me.f * CTX + me.c
    take = me.c * FSDP + me.f
    moving = give != take
    barrier = pltpu.get_barrier_semaphore()

    @pl.when(moving)
    def _():
        pl.semaphore_signal(
            barrier, inc=1, device_id=(take % CTX, take // CTX), device_id_type=MESH
        )

    friends = [sibling] + [p[0] for p in planes[1:]] + line[1:]
    greet(friends, jnp.where(moving, 1, 0))
    move = send(g, rows_in, ms.at[0], mr.at[0], (give // FSDP, give % FSDP))

    grad = g[...]
    parts = [
        jnp.concatenate([p.astype(f32), jnp.zeros((8, KV), f32)], axis=0).astype(bf16)
        for p in split(grad, 3)
    ]
    left = jnp.concatenate([parts[i] for i, _ in PAIRS[6]], axis=0)
    right = jnp.concatenate([parts[j] for _, j in PAIRS[6]], axis=0)
    local = tn(left, right)
    for i, (r, s) in enumerate(TRI[:14]):
        width = min(128, KV - s * 128)
        pack[i * 128 : i * 128 + 128, :width] = local[r * 128 : r * 128 + 128, s * 128 : s * 128 + width]
    pack[1792:1856, :64] = local[512:, 512:]
    pack[1856:, :] = jnp.zeros((PACKED - 1856, 128), f32)

    half = PACKED // 2
    unit = half // 16
    small = unit // 4

    def rows(start, size):
        return pl.ds(pl.multiple_of(start, 8), size)

    copies = []
    swap = send(pack.at[rows((1 - k) * half, half)], core_in, cs.at[0], cr.at[0], sibling)
    swap.start()

    @pl.when(moving)
    def _():
        move.start()

    @pl.when(jnp.logical_not(moving))
    def _():
        rows_in[...] = grad

    swap.wait_recv()
    acc[...] = pack[rows(k * half, half), :] + core_in[...]
    copies.append(swap)
    mine = y * 4 + z
    first = []
    for n in range(1, 16):
        device, index = planes[n]
        copy = send(acc.at[rows(index * unit, unit)], yz_in.at[n], ys.at[n], yr.at[n], device)
        copy.start()
        first.append(copy)
    total = acc[rows(mine * unit, unit), :]
    for n in range(1, 16):
        first[n - 1].wait_recv()
        total = total + yz_in[n]
    yz_in[0] = total
    second = []
    for s in range(1, 4):
        to = (x + s) % 4
        copy = send(yz_in.at[0, rows(to * small, small)], x_in.at[s], xs.at[s], xr.at[s], line[s])
        copy.start()
        second.append(copy)
    total = yz_in[0, rows(x * small, small), :]
    for s in range(1, 4):
        second[s - 1].wait_recv()
        total = total + x_in[s]
    base = k * half + mine * unit
    gram[rows(base + x * small, small), :] = total
    third = []
    for s in range(1, 4):
        there = gram.at[rows(base + x * small, small)]
        copy = send(there, there, xs2.at[s], xr2.at[s], line[s])
        copy.start()
        third.append(copy)
    for copy in third:
        copy.wait_recv()
    fourth = []
    for n in range(1, 16):
        there = gram.at[rows(base, unit)]
        copy = send(there, there, ys2.at[n], yr2.at[n], planes[n][0])
        copy.start()
        fourth.append(copy)
    for copy in fourth:
        copy.wait_recv()
    there = gram.at[rows(k * half, half)]
    last = send(there, there, cs2.at[0], cr2.at[0], sibling)
    last.start()
    last.wait_recv()
    copies += first + second + third + fourth + [last]

    blocks = {}
    for i, (r, s) in enumerate(TRI):
        if i < 14:
            blocks[r, s] = gram[i * 128 : i * 128 + 128, :]
            if r != s:
                blocks[s, r] = blocks[r, s].T
    edge = gram[1792:1856, :]
    lines = []
    for r in range(4):
        lines.append(jnp.concatenate([blocks[r, s] for s in range(5)], axis=1)[:, :KV])
    bottom = [blocks[4, s][:64] for s in range(4)] + [edge]
    lines.append(jnp.concatenate(bottom, axis=1)[:, :KV])
    full = jnp.concatenate(lines, axis=0)
    row = lax.broadcasted_iota(jnp.int32, (KV, KV), 0)
    col = lax.broadcasted_iota(jnp.int32, (KV, KV), 1)
    diagonal = row == col
    squares = jnp.sum(jnp.where(diagonal, full, 0.0))
    norm = jnp.sqrt(jnp.full((1, 1), squares, f32)) + 1e-07
    inv = 1.0 / norm
    a_scr[...] = full * inv * inv

    @pl.when(moving)
    def _():
        move.wait_recv()

    out[...] = rows_in[...] * inv

    def lay_left(ref, value, terms):
        parts = split(value, 3 if terms == 6 else 2)
        for t, (i, _) in enumerate(PAIRS[terms]):
            ref[:, t * LAT : (t + 1) * LAT] = parts[i][:, :LAT]
            at = terms * LAT + t * ROPE
            ref[:, at : at + ROPE] = parts[i][:, LAT:]

    def lay_right(value, terms):
        parts = split(value, 3 if terms == 6 else 2)
        for t, (_, j) in enumerate(PAIRS[terms]):
            right_scr[t * LAT : (t + 1) * LAT, :] = parts[j][:LAT]
            at = terms * LAT + t * ROPE
            right_scr[at : at + ROPE, :] = parts[j][LAT:]

    def symmetric(terms):
        size = terms * KV
        wide = nn(left_scr[:, :size], right_scr[:size, :LAT])
        corner = nn(left_scr[LAT:, :size], right_scr[:size, LAT:])
        return jnp.concatenate([wide, jnp.concatenate([wide[LAT:].T, corner], axis=0)], axis=1)

    def mix(terms):
        a = a_scr[...]
        lay_left(left_scr, a, terms)
        lay_right(a, terms)
        mixing = quintic_b * a + quintic_c * symmetric(terms)
        lay_right(mixing, terms)
        lay_left(thin_scr, out[...], terms)
        size = terms * KV
        out[...] = quintic_a * out[...] + nn(thin_scr[:, :size], right_scr[:size, :])

    def advance(terms):
        b = quintic_a * a_scr[...] + symmetric(terms)
        lay_left(left_scr, b, terms)
        a_scr[...] = quintic_a * b + symmetric(terms)

    mix(6)
    advance(6)

    def iteration(step, _):
        mix(3)

        @pl.when(step < NS_ITERS - 1)
        def _():
            advance(3)

        return 0

    lax.fori_loop(1, NS_ITERS, iteration, 0)
    iterate = out[...]
    out[...] = iterate * (0.2 * math.sqrt(D))

    @pl.when(moving)
    def _():
        move.wait_send()

    for copy in copies:
        copy.wait_send()


def muon(g):
    half = PACKED // 2
    sems = [1, 1, 16, 16, 4, 4, 4, 4, 16, 16, 1, 1]
    return pl.pallas_call(
        muon_kernel,
        out_shape=jax.ShapeDtypeStruct((PIECE, KV), f32),
        in_specs=[VMEM],
        out_specs=VMEM,
        scratch_shapes=[
            pltpu.VMEM((PACKED, 128), f32),
            pltpu.VMEM((half, 128), f32),
            pltpu.VMEM((16, half // 16, 128), f32),
            pltpu.VMEM((4, half // 64, 128), f32),
            pltpu.VMEM((half, 128), f32),
            pltpu.VMEM((PACKED, 128), f32),
            pltpu.VMEM((PIECE, KV), f32),
            pltpu.VMEM((KV, KV), f32),
            pltpu.VMEM((KV, 6 * KV), bf16),
            pltpu.VMEM((PIECE, 6 * KV), bf16),
            pltpu.VMEM((6 * KV, KV), bf16),
            pltpu.SemaphoreType.DMA((1,)),
            pltpu.SemaphoreType.DMA((1,)),
        ]
        + [pltpu.SemaphoreType.DMA((n,)) for n in sems],
        compiler_params=pltpu.CompilerParams(
            collective_id=2, has_side_effects=True, vmem_limit_bytes=32 * MiB
        ),
        name="muon",
    )(g)


def per_device(tokens, kv_weight, latent_gain, queries, out_grad, segment_ids):
    tok = tokens[0]
    c = lax.axis_index("ctx")
    positions = c * BLOCK + jnp.arange(BLOCK, dtype=jnp.int32)
    cos, sin = rope_tables(positions)
    gain = latent_gain[None]
    docs = segment_ids[0]
    lanes = jnp.arange(ROPE, dtype=jnp.int32)
    hot = (docs[:, None] == lanes[None]).astype(f32)
    qt = jnp.transpose(queries[0], (1, 2, 0))
    keys, proj, q = make_keys(tok, kv_weight.T, gain, hot, cos, sin, qt)
    keys = keys.reshape(WINDOW, PAD)
    dout = out_grad[0].reshape(BLOCK * HEADS, LAT)
    attended, kg, peak = attention(q, dout, hot, keys)
    rows, top = weight_grad(
        kg.reshape(SLOTS, BLOCK, KV), proj, gain, cos, sin, tok, peak
    )
    update = muon(rows)
    return (attended.reshape(1, BLOCK, HEADS, LAT), jnp.max(top.reshape(TILE_Q, HEADS), axis=0), update)


def solution(mesh):
    return jax.shard_map(
        per_device,
        mesh=mesh,
        in_specs=(
            P("fsdp", "ctx", None),
            P("fsdp", None),
            P(),
            P("fsdp", "ctx", None, None),
            P("fsdp", "ctx", None, None),
            P("fsdp", "ctx"),
        ),
        out_specs=(P("fsdp", "ctx", None, None), P(), P(("ctx", "fsdp"), None)),
        check_vma=False,
    )
```

profile of v0, /device:TPU:1, one launch (start us, length us, event | category | flops | bytes accessed | tf_op | source)
XLA Modules:
  0.0 264.7 jit_solution(5900239159689206111)
XLA Ops:
  0.7 0.7 fusion.hot
  1.4 0.3 multiply_sine_fusion
  1.7 0.0 copy-start
  1.7 1.5 copy-done
  3.2 0.0 copy-start.1
  3.2 1.2 copy-done.1
  4.4 0.0 copy-start.2
  4.4 0.7 copy-done.2
  5.1 0.0 copy-start.4
  5.1 59.7 %keys.1 = (bf16[9,128,640]{2,1,0:T(8,128)(2,1)S(1)}, f32[128,576]{1,0:T(8,128)S(1)}, bf16[4096,576]{1,0:T(8,128)(2,1)}) custom-call(bf16[128,7168]{1,0:T(8,128)(2,1)S(1)} %bitcast.11, bf16[576,896]{1,0:T(8,128)(2,1)S(1)} %bitcast.14, f32[1,512]{1,0:T(1,128)S(1)} %bitcast.15, f32[128,64]{1,0:T(8,128)S(1)} %fusion.hot, f32[128,32]{1,0:T(8,128)S(1)} %get-tuple-element.20.cos, ...), custom_call_target="tpu_custom_call" | custom-call | tf_op jit(solution)/shard_map/keys/pallas_call | solution.py:290
  64.9 0.0 copy-done.4
  64.9 0.0 copy-start.3
  64.9 2.5 copy-done.3
  67.4 40.0 %attention.1 = (bf16[4096,512]{1,0:T(8,128)(2,1)}, f32[1152,576]{1,0:T(8,128)S(1)}, f32[8,512]{1,0:T(8,128)S(1)}) custom-call(bf16[4096,576]{1,0:T(8,128)(2,1)S(1)} %copy-done.3, bf16[4096,512]{1,0:T(8,128)(2,1)S(1)} %bitcast.17, f32[128,64]{1,0:T(8,128)S(1)} %fusion.hot, bf16[1152,640]{1,0:T(8,128)(2,1)S(1)} %bitcast.18), custom_call_target="tpu_custom_call" | custom-call | flops 12683575296 | bytes 16777216 | tf_op jit(solution)/shard_map/attention/pallas_call | solution.py:370
  107.4 88.4 %weight_grad.1 = (f32[56,576]{1,0:T(8,128)S(1)}, f32[8,64]{1,0:T(8,128)S(1)}) custom-call(f32[9,128,576]{2,1,0:T(8,128)S(1)} %bitcast.13, f32[128,576]{1,0:T(8,128)S(1)} %get-tuple-element.15.proj, f32[1,512]{1,0:T(1,128)S(1)} %bitcast.16, f32[128,32]{1,0:T(8,128)S(1)} %get-tuple-element.20.cos, f32[128,32]{1,0:T(8,128)S(1)} %get-tuple-element.19.sin, ...), custom_call_target="tpu_custom_call" | custom-call | tf_op jit(solution)/shard_map/weight_grad/pallas_call | solution.py:529
  195.8 0.1 reshape.32
  195.9 0.5 reduce_max.9
  196.4 67.6 %muon.1 = f32[56,576]{1,0:T(8,128)S(1)} custom-call(f32[56,576]{1,0:T(8,128)S(1)} %get-tuple-element.18.g), custom_call_target="tpu_custom_call" | custom-call | tf_op jit(solution)/shard_map/muon/pallas_call | solution.py:772
  264.0 0.7 copy.10
  (2 shorter events, 0.0 us)
Async XLA Ops:
  1.7 1.5 copy-start
  3.2 1.2 copy-start.1
  4.4 0.7 copy-start.2
  5.1 59.7 %copy-start.4 = (bf16[1,128,32,512]{3,2,1,0:T(8,128)(2,1)S(1)}, bf16[1,128,32,512]{3,2,1,0:T(8,128)(2,1)}, u32[]{:S(2)}) copy-start(bf16[1,128,32,512]{3,2,1,0:T(8,128)(2,1)} %param.10) | copy-start | bytes 12582916
  64.9 2.5 copy-start.3
where the time goes:
time: 265 us
  Pallas kernels  256 us (97%)
  local copies, waits for them, and re-layouts  6.61 us (2%)
    pallas_call x1, Pallas kernels, weight_grad(): pl.pallas_call(grads_kernel, out_shape=(jax.ShapeDtypeStruct((PIECE, KV),...  88.4 us
    pallas_call x1, Pallas kernels, muon(): pl.pallas_call(muon_kernel, out_shape=jax.ShapeDtypeStruct((PIECE, KV), f...  67.6 us
    pallas_call x1, Pallas kernels, make_keys(): pl.pallas_call(keys_kernel, out_shape=(jax.ShapeDtypeStruct((SLOTS, BLOCK...  59.7 us
    pallas_call x1, Pallas kernels, attention(): pl.pallas_call(attention_kernel, grid=(TILES,), in_specs=[per_tile(KV), p...  40 us
    unnamed x11, local copies, waits for them, and re-layouts  6.54 us

commit v1 on v0

--- a/solution.py
+++ b/solution.py
@@ -38,7 +38,7 @@
 
 MESH = pl.DeviceIdType.MESH
 VMEM = pl.BlockSpec(memory_space=pltpu.VMEM)
-ANY = pl.BlockSpec(memory_space=pl.ANY)
+HBM = pl.BlockSpec(memory_space=pltpu.HBM)
 f32, bf16 = jnp.float32, jnp.bfloat16
 
 
@@ -294,7 +294,7 @@
             jax.ShapeDtypeStruct((BLOCK, KV), f32),
             jax.ShapeDtypeStruct((BLOCK * HEADS, KV), bf16),
         ),
-        in_specs=[ANY, ANY] + [VMEM] * 4 + [ANY],
+        in_specs=[HBM, HBM] + [VMEM] * 4 + [HBM],
         out_specs=(VMEM,) * 3,
         scratch_shapes=[
             pltpu.VMEM((FSDP, KV, SHARD), bf16),
@@ -309,7 +309,7 @@
             pltpu.SemaphoreType.DMA((8,)),
         ],
         compiler_params=pltpu.CompilerParams(
-            collective_id=0, has_side_effects=True, vmem_limit_bytes=48 * MiB
+            collective_id=0, has_side_effects=True, vmem_limit_bytes=58 * MiB
         ),
         name="keys",
     )(tok, w, gain, hot, cos, sin, qt)
@@ -390,7 +390,7 @@
             jax.ShapeDtypeStruct((8, ROWS), f32),
         ),
         compiler_params=pltpu.CompilerParams(
-            dimension_semantics=("arbitrary",), vmem_limit_bytes=32 * MiB
+            dimension_semantics=("arbitrary",), vmem_limit_bytes=50 * MiB
         ),
         cost_estimate=pl.CostEstimate(
             flops=flops, bytes_accessed=16 << 20, transcendentals=BLOCK * HEADS * WINDOW
@@ -409,7 +409,6 @@
     sibling = me.at(k=1 - k)
     back = [me.ctx((c - 2 * j + CTX) % CTX) for j in range(1, 8)]
     peers = [me.fsdp((f + s) % FSDP) for s in range(1, FSDP)]
-    greet([sibling] + back + peers)
 
     def slot(distance):
         return SLOTS - 1 - distance
@@ -524,37 +523,7 @@
         copy.wait_send()
 
 
-def weight_grad(kg, proj, gain, cos, sin, tok, peak):
-    sems = [4, 4, 4, 4, 7, 7, 7, 7, 8, 8, 8, 8, 7, 7]
-    return pl.pallas_call(
-        grads_kernel,
-        out_shape=(
-            jax.ShapeDtypeStruct((PIECE, KV), f32),
-            jax.ShapeDtypeStruct((8, ROPE), f32),
-        ),
-        in_specs=[VMEM] * 7,
-        out_specs=(VMEM, VMEM),
-        scratch_shapes=[
-            pltpu.VMEM((4, BLOCK, KV), f32),
-            pltpu.VMEM((4, BLOCK, KV), f32),
-            pltpu.VMEM((4, BLOCK, KV), f32),
-            pltpu.VMEM((FSDP, BLOCK, KV), bf16),
-            pltpu.VMEM((FSDP, 8, ROWS), f32),
-            pltpu.VMEM((FSDP, BLOCK, SHARD), bf16),
-            pltpu.VMEM((SHARD, FSDP * BLOCK), bf16),
-            pltpu.VMEM((CTX, PIECE, PAD), f32),
-            pltpu.VMEM((CTX // 2, PIECE, PAD), f32),
-            pltpu.VMEM((CTX // 2, PIECE, PAD), f32),
-            pltpu.VMEM((CTX // 2, PIECE, PAD), f32),
-        ]
-        + [pltpu.SemaphoreType.DMA((n,)) for n in sems],
-        compiler_params=pltpu.CompilerParams(
-            collective_id=1, has_side_effects=True, vmem_limit_bytes=32 * MiB
-        ),
-        name="weight_grad",
-    )(kg, proj, gain, cos, sin, tok, peak)
-
-
+GRADS = 25
 TRI = [(r, s) for r in range(5) for s in range(r, 5)]
 PACKED = 2048
 PAIRS = {3: [(0, 0), (0, 1), (1, 0)], 6: [(0, 0), (0, 1), (1, 0), (0, 2), (2, 0), (1, 1)]}
@@ -586,16 +555,6 @@
     give = me.f * CTX + me.c
     take = me.c * FSDP + me.f
     moving = give != take
-    barrier = pltpu.get_barrier_semaphore()
-
-    @pl.when(moving)
-    def _():
-        pl.semaphore_signal(
-            barrier, inc=1, device_id=(take % CTX, take // CTX), device_id_type=MESH
-        )
-
-    friends = [sibling] + [p[0] for p in planes[1:]] + line[1:]
-    greet(friends, jnp.where(moving, 1, 0))
     move = send(g, rows_in, ms.at[0], mr.at[0], (give // FSDP, give % FSDP))
 
     grad = g[...]
@@ -766,35 +725,77 @@
         copy.wait_send()
 
 
-def muon(g):
+def update_kernel(kg, proj, gain, cos, sin, tok, peak, out, peak_out, rows, *scratch):
+    me = Place()
+    give, take = me.f * CTX + me.c, me.c * FSDP + me.f
+    moving = give != take
+
+    @pl.when(moving)
+    def _():
+        pl.semaphore_signal(
+            pltpu.get_barrier_semaphore(),
+            inc=1,
+            device_id=(take % CTX, take // CTX),
+            device_id_type=MESH,
+        )
+
+    c, x, y, z = me.c, me.x, me.y, me.zh * 2 + me.zl
+    friends = [me.at(k=1 - me.k)]
+    friends += [me.ctx((c - 2 * j + CTX) % CTX) for j in range(1, 8)]
+    friends += [me.fsdp((me.f + s) % FSDP) for s in range(1, FSDP)]
+    for n in range(1, 16):
+        zz = (z + n % 4) % 4
+        friends.append(me.at(y=(y + n // 4) % 4, zh=zz // 2, zl=zz % 2))
+    friends += [me.at(x=(x + s) % 4) for s in range(1, 4)]
+    greet(friends, jnp.where(moving, 1, 0))
+    grads_kernel(kg, proj, gain, cos, sin, tok, peak, rows, peak_out, *scratch[:GRADS])
+    muon_kernel(rows, out, *scratch[GRADS:])
+
+
+def weight_update(kg, proj, gain, cos, sin, tok, peak):
     half = PACKED // 2
-    sems = [1, 1, 16, 16, 4, 4, 4, 4, 16, 16, 1, 1]
+    dma = lambda sizes: [pltpu.SemaphoreType.DMA((n,)) for n in sizes]
+    grads = [
+        pltpu.VMEM((4, BLOCK, KV), f32),
+        pltpu.VMEM((4, BLOCK, KV), f32),
+        pltpu.VMEM((4, BLOCK, KV), f32),
+        pltpu.VMEM((FSDP, BLOCK, KV), bf16),
+        pltpu.VMEM((FSDP, 8, ROWS), f32),
+        pltpu.VMEM((FSDP, BLOCK, SHARD), bf16),
+        pltpu.VMEM((SHARD, FSDP * BLOCK), bf16),
+        pltpu.VMEM((CTX, PIECE, PAD), f32),
+        pltpu.VMEM((CTX // 2, PIECE, PAD), f32),
+        pltpu.VMEM((CTX // 2, PIECE, PAD), f32),
+        pltpu.VMEM((CTX // 2, PIECE, PAD), f32),
+    ] + dma([4, 4, 4, 4, 7, 7, 7, 7, 8, 8, 8, 8, 7, 7])
+    assert len(grads) == GRADS
+    newton = [
+        pltpu.VMEM((PACKED, 128), f32),
+        pltpu.VMEM((half, 128), f32),
+        pltpu.VMEM((16, half // 16, 128), f32),
+        pltpu.VMEM((4, half // 64, 128), f32),
+        pltpu.VMEM((half, 128), f32),
+        pltpu.VMEM((PACKED, 128), f32),
+        pltpu.VMEM((PIECE, KV), f32),
+        pltpu.VMEM((KV, KV), f32),
+        pltpu.VMEM((KV, 6 * KV), bf16),
+        pltpu.VMEM((PIECE, 6 * KV), bf16),
+        pltpu.VMEM((6 * KV, KV), bf16),
+    ] + dma([1, 1, 1, 1, 16, 16, 4, 4, 4, 4, 16, 16, 1, 1])
     return pl.pallas_call(
-        muon_kernel,
-        out_shape=jax.ShapeDtypeStruct((PIECE, KV), f32),
-        in_specs=[VMEM],
-        out_specs=VMEM,
-        scratch_shapes=[
-            pltpu.VMEM((PACKED, 128), f32),
-            pltpu.VMEM((half, 128), f32),
-            pltpu.VMEM((16, half // 16, 128), f32),
-            pltpu.VMEM((4, half // 64, 128), f32),
-            pltpu.VMEM((half, 128), f32),
-            pltpu.VMEM((PACKED, 128), f32),
-            pltpu.VMEM((PIECE, KV), f32),
-            pltpu.VMEM((KV, KV), f32),
-            pltpu.VMEM((KV, 6 * KV), bf16),
-            pltpu.VMEM((PIECE, 6 * KV), bf16),
-            pltpu.VMEM((6 * KV, KV), bf16),
-            pltpu.SemaphoreType.DMA((1,)),
-            pltpu.SemaphoreType.DMA((1,)),
-        ]
-        + [pltpu.SemaphoreType.DMA((n,)) for n in sems],
+        update_kernel,
+        out_shape=(
+            jax.ShapeDtypeStruct((PIECE, KV), f32),
+            jax.ShapeDtypeStruct((8, ROPE), f32),
+        ),
+        in_specs=[VMEM] * 7,
+        out_specs=(VMEM, VMEM),
+        scratch_shapes=[pltpu.VMEM((PIECE, KV), f32)] + grads + newton,
         compiler_params=pltpu.CompilerParams(
-            collective_id=2, has_side_effects=True, vmem_limit_bytes=32 * MiB
+            collective_id=1, has_side_effects=True, vmem_limit_bytes=48 * MiB
         ),
-        name="muon",
-    )(g)
+        name="weight_grad",
+    )(kg, proj, gain, cos, sin, tok, peak)
 
 
 def per_device(tokens, kv_weight, latent_gain, queries, out_grad, segment_ids):
@@ -811,10 +812,9 @@
     keys = keys.reshape(WINDOW, PAD)
     dout = out_grad[0].reshape(BLOCK * HEADS, LAT)
     attended, kg, peak = attention(q, dout, hot, keys)
-    rows, top = weight_grad(
+    update, top = weight_update(
         kg.reshape(SLOTS, BLOCK, KV), proj, gain, cos, sin, tok, peak
     )
-    update = muon(rows)
     return (attended.reshape(1, BLOCK, HEADS, LAT), jnp.max(top.reshape(TILE_Q, HEADS), axis=0), update)
 
 

time: 265 us -> 263 us (level)
  local copies, waits for them, and re-layouts: 6.61 us -> 3.95 us
    pallas_call x2 -> x1, Pallas kernels: 156 us -> 152 us  [weight_update(): pl.pallas_call(update_kernel, out_shape=(jax.ShapeDtypeStruct((PIECE, KV)...]
    pallas_call x1, Pallas kernels: 40 us -> 42.7 us  [attention(): pl.pallas_call(attention_kernel, grid=(TILES,), in_specs=[per_tile(KV), p...]
    unnamed x11 -> x17, local copies, waits for them, and re-layouts: 6.54 us -> 3.88 us
where the time goes in v1:
time: 263 us
  Pallas kernels  255 us (97%)
  local copies, waits for them, and re-layouts  3.95 us (2%)
  other arithmetic  2.88 us (1%)
    pallas_call x1, Pallas kernels, weight_update(): pl.pallas_call(update_kernel, out_shape=(jax.ShapeDtypeStruct((PIECE, KV)...  152 us
    pallas_call x1, Pallas kernels, make_keys(): pl.pallas_call(keys_kernel, out_shape=(jax.ShapeDtypeStruct((SLOTS, BLOCK...  61.2 us
    pallas_call x1, Pallas kernels, attention(): pl.pallas_call(attention_kernel, grid=(TILES,), in_specs=[per_tile(KV), p...  42.7 us

profile of v1, /device:TPU:1, one launch (start us, length us, event | category | flops | bytes accessed | tf_op | source)
XLA Modules:
  0.0 263.0 jit_solution(1885269456261067495)
XLA Ops:
  0.7 1.4 fusion.hot
  2.0 0.0 copy-start.5
  2.0 1.0 multiply_sine_fusion
  3.0 61.2 %keys.1 = (bf16[9,128,640]{2,1,0:T(8,128)(2,1)}, f32[128,576]{1,0:T(8,128)}, bf16[4096,576]{1,0:T(8,128)(2,1)}) custom-call(bf16[128,7168]{1,0:T(8,128)(2,1)} %bitcast.11, bf16[576,896]{1,0:T(8,128)(2,1)} %bitcast.18, f32[1,512]{1,0:T(1,128)} %bitcast.14, f32[128,64]{1,0:T(8,128)} %fusion.hot, f32[128,32]{1,0:T(8,128)} %get-tuple-element.20.cos, ...), custom_call_target="tpu_custom_call" | custom-call | tf_op jit(solution)/shard_map/keys/pallas_call | solution.py:290
  64.2 0.0 copy-done.5
  64.2 0.0 copy-start.7
  64.2 1.4 copy-done.7
  65.6 0.0 copy-start
  65.6 0.0 copy-start.2
  65.6 0.0 copy-start.3
  65.6 0.0 copy-start.4
  65.6 0.0 copy-start.6
  65.6 42.7 %attention.1 = (bf16[4096,512]{1,0:T(8,128)(2,1)}, f32[1152,576]{1,0:T(8,128)}, f32[8,512]{1,0:T(8,128)S(1)}) custom-call(bf16[4096,576]{1,0:T(8,128)(2,1)} %get-tuple-element.11.q, bf16[4096,512]{1,0:T(8,128)(2,1)} %bitcast.20, f32[128,64]{1,0:T(8,128)S(1)} %copy-done.5, bf16[1152,640]{1,0:T(8,128)(2,1)S(1)} %bitcast.16), custom_call_target="tpu_custom_call" | custom-call | flops 12683575296 | bytes 16777216 | tf_op jit(solution)/shard_map/attention/pallas_call | solution.py:370
  108.3 0.0 copy-done
  108.3 0.0 copy-done.2
  108.3 0.0 copy-done.3
  108.3 0.0 copy-done.4
  108.3 0.0 copy-done.6
  108.3 0.0 copy-start.1
  108.4 1.8 copy-done.1
  110.2 151.5 %weight_grad.1 = (f32[56,576]{1,0:T(8,128)S(1)}, f32[8,64]{1,0:T(8,128)S(1)}) custom-call(f32[9,128,576]{2,1,0:T(8,128)S(1)} %bitcast.13, f32[128,576]{1,0:T(8,128)S(1)} %copy-done.4, f32[1,512]{1,0:T(1,128)S(1)} %bitcast.15, f32[128,32]{1,0:T(8,128)S(1)} %copy-done.3, f32[128,32]{1,0:T(8,128)S(1)} %copy-done.2, bf16[128,7168]{1,0:T(8,128)(2,1)S(1)} %bitcast.12, ...), custom_call_target="tpu_custom_call" | custom-call | tf_op jit(solution)/shard_map/weight_grad/pallas_call | solution.py:785
  261.7 0.1 reshape.32
  261.8 0.5 reduce_max.9
  262.3 0.7 copy.10
  (2 shorter events, 0.0 us)
Async XLA Ops:
  2.0 62.2 %copy-start.5 = (f32[128,64]{1,0:T(8,128)S(1)}, f32[128,64]{1,0:T(8,128)}, u32[]{:S(2)}) copy-start(f32[128,64]{1,0:T(8,128)} %fusion.hot) | copy-start | bytes 98308
  64.2 1.4 copy-start.7
  65.6 42.7 %copy-start = (bf16[1,128,7168]{2,1,0:T(8,128)(2,1)S(1)}, bf16[1,128,7168]{2,1,0:T(8,128)(2,1)}, u32[]{:S(2)}) copy-start(bf16[1,128,7168]{2,1,0:T(8,128)(2,1)} %param.6) | copy-start | bytes 5505028
  65.6 42.7 %copy-start.2 = (f32[128,32]{1,0:T(8,128)S(1)}, f32[128,32]{1,0:T(8,128)}, u32[]{:S(2)}) copy-start(f32[128,32]{1,0:T(8,128)} %get-tuple-element.19.sin) | copy-start | bytes 49156
  65.6 42.7 %copy-start.3 = (f32[128,32]{1,0:T(8,128)S(1)}, f32[128,32]{1,0:T(8,128)}, u32[]{:S(2)}) copy-start(f32[128,32]{1,0:T(8,128)} %get-tuple-element.20.cos) | copy-start | bytes 49156
  65.6 42.7 %copy-start.4 = (f32[128,576]{1,0:T(8,128)S(1)}, f32[128,576]{1,0:T(8,128)}, u32[]{:S(2)}) copy-start(f32[128,576]{1,0:T(8,128)} %get-tuple-element.15.proj) | copy-start | bytes 884740
  65.6 42.7 %copy-start.6 = (f32[512]{0:T(512)S(1)}, f32[512]{0:T(512)}, u32[]{:S(2)}) copy-start(f32[512]{0:T(512)} %param.8) | copy-start | bytes 6148
  108.3 1.8 copy-start.1

commit v2 on v1

--- a/solution.py
+++ b/solution.py
@@ -178,7 +178,7 @@
             qrow[lanes, pl.ds(h, BLOCK, stride=HEADS), :] = block.T
         return 0
 
-    lax.fori_loop(0, HEADS // 2, turn, 0)
+    lax.fori_loop(0, 10, turn, 0)
 
     prev0 = forward(up[0], f_prev, 0)
     relay_up = post(f_prev, wall, k, 0, x_up)
@@ -186,14 +186,17 @@
     relay_down = post(f_next, wall, k, 1, x_down)
     posted.extend([relay_up, relay_down])
     s_own = [pass_on(own_z[q], o_own, q) for q in range(2)]
-    lax.fori_loop(HEADS // 2, HEADS, turn, 0)
+    lax.fori_loop(10, 22, turn, 0)
+    prev1 = forward(up[1], f_prev, 1)
+    next0 = forward(down[1], f_next, 0)
+    lax.fori_loop(22, HEADS, turn, 0)
+    far0 = forward(relay_up, f_far, 0)
+    far1 = forward(relay_down, f_far, 1)
+    s_prev0 = pass_on(prev0[0], o_prev, 0)
+    s_next1 = pass_on(next1[0], o_next, 1)
     fetch_w.wait()
     fetch_tok.wait()
     acc = nt(tok[:, pl.ds(pl.multiple_of(own * SHARD, 128), SHARD)], wall[own])
-    prev1 = forward(up[1], f_prev, 1)
-    next0 = forward(down[1], f_next, 0)
-    s_prev0 = pass_on(prev0[0], o_prev, 0)
-    s_next1 = pass_on(next1[0], o_next, 1)
 
     def narrow(i, _):
         rows = pl.ds(pl.multiple_of(i * ROWS, ROWS), ROWS)
@@ -206,8 +209,6 @@
     for copy in s_own:
         copy.wait_recv()
     acc = add(acc, o_own)
-    far0 = forward(relay_up, f_far, 0)
-    far1 = forward(relay_down, f_far, 1)
     prev0[1].wait_recv()
     prev1[1].wait_recv()
     acc = add(acc, f_prev)
@@ -418,12 +419,6 @@
         copy = send(kg.at[slot(2 * n + 1)], near.at[n], ns.at[n], nr.at[n], sibling)
         copy.start()
         swaps.append(copy)
-    tokens = []
-    for s in range(1, FSDP):
-        columns = pl.ds(pl.multiple_of(((f + s) % FSDP) * SHARD, 128), SHARD)
-        copy = send(tok.at[:, columns], tok_in.at[s], as_.at[s - 1], ar.at[s - 1], peers[s - 1])
-        copy.start()
-        tokens.append(copy)
     gathers = []
     for s in range(1, FSDP):
         copy = send(peak, peaks.at[s], ps.at[s - 1], pr.at[s - 1], peers[s - 1])
@@ -450,10 +445,12 @@
         copy = send(outbox.at[n], far.at[n], fs.at[n], fr.at[n], back[n])
         copy.start()
         sends.append(copy)
-    tok_t[:, :BLOCK] = tok[:, pl.ds(pl.multiple_of(f * SHARD, 128), SHARD)].T
+    tokens = []
     for s in range(1, FSDP):
-        tokens[s - 1].wait_recv()
-        tok_t[:, s * BLOCK : (s + 1) * BLOCK] = tok_in[s].T
+        columns = pl.ds(pl.multiple_of(((f + s) % FSDP) * SHARD, 128), SHARD)
+        copy = send(tok.at[:, columns], tok_in.at[s], as_.at[s - 1], ar.at[s - 1], peers[s - 1])
+        copy.start()
+        tokens.append(copy)
     for copy in sends:
         copy.wait_recv()
     key_grad = own
@@ -475,6 +472,10 @@
         copy = send(kvg.at[0], kvg.at[s], gs.at[s - 1], gr.at[s - 1], peers[s - 1])
         copy.start()
         spread.append(copy)
+    tok_t[:, :BLOCK] = tok[:, pl.ds(pl.multiple_of(f * SHARD, 128), SHARD)].T
+    for s in range(1, FSDP):
+        tokens[s - 1].wait_recv()
+        tok_t[:, s * BLOCK : (s + 1) * BLOCK] = tok_in[s].T
     top = peak[...]
     for s in range(1, FSDP):
         gathers[s - 1].wait_recv()

time: 263 us -> 260 us (0.989)
  Pallas kernels: 255 us -> 252 us
    pallas_call x1, Pallas kernels: 61.2 us -> 57.5 us  [make_keys(): pl.pallas_call(keys_kernel, out_shape=(jax.ShapeDtypeStruct((SLOTS, BLOCK...]
where the time goes in v2:
time: 260 us; the launch traced here: 259 us
  Pallas kernels  252 us (97%)
  local copies, waits for them, and re-layouts  3.95 us (2%)
  other arithmetic  2.88 us (1%)
    pallas_call x1, Pallas kernels, weight_update(): pl.pallas_call(update_kernel, out_shape=(jax.ShapeDtypeStruct((PIECE, KV)...  151 us
    pallas_call x1, Pallas kernels, make_keys(): pl.pallas_call(keys_kernel, out_shape=(jax.ShapeDtypeStruct((SLOTS, BLOCK...  57.5 us
    pallas_call x1, Pallas kernels, attention(): pl.pallas_call(attention_kernel, grid=(TILES,), in_specs=[per_tile(KV), p...  42.7 us

profile of v2, /device:TPU:1, one launch (start us, length us, event | category | flops | bytes accessed | tf_op | source)
XLA Modules:
  0.0 259.3 jit_solution(10464119311322603164)
XLA Ops:
  0.7 1.4 fusion.hot
  2.0 0.0 copy-start.5
  2.0 1.0 multiply_sine_fusion
  3.0 57.5 %keys.1 = (bf16[9,128,640]{2,1,0:T(8,128)(2,1)}, f32[128,576]{1,0:T(8,128)}, bf16[4096,576]{1,0:T(8,128)(2,1)}) custom-call(bf16[128,7168]{1,0:T(8,128)(2,1)} %bitcast.11, bf16[576,896]{1,0:T(8,128)(2,1)} %bitcast.18, f32[1,512]{1,0:T(1,128)} %bitcast.14, f32[128,64]{1,0:T(8,128)} %fusion.hot, f32[128,32]{1,0:T(8,128)} %get-tuple-element.20.cos, ...), custom_call_target="tpu_custom_call" | custom-call | tf_op jit(solution)/shard_map/keys/pallas_call | solution.py:291
  60.6 0.0 copy-done.5
  60.6 0.0 copy-start.7
  60.6 1.4 copy-done.7
  61.9 0.0 copy-start
  61.9 0.0 copy-start.2
  61.9 0.0 copy-start.3
  61.9 0.0 copy-start.4
  61.9 0.0 copy-start.6
  62.0 42.7 %attention.1 = (bf16[4096,512]{1,0:T(8,128)(2,1)}, f32[1152,576]{1,0:T(8,128)}, f32[8,512]{1,0:T(8,128)S(1)}) custom-call(bf16[4096,576]{1,0:T(8,128)(2,1)} %get-tuple-element.11.q, bf16[4096,512]{1,0:T(8,128)(2,1)} %bitcast.20, f32[128,64]{1,0:T(8,128)S(1)} %copy-done.5, bf16[1152,640]{1,0:T(8,128)(2,1)S(1)} %bitcast.16), custom_call_target="tpu_custom_call" | custom-call | flops 12683575296 | bytes 16777216 | tf_op jit(solution)/shard_map/attention/pallas_call | solution.py:371
  104.7 0.0 copy-done
  104.7 0.0 copy-done.2
  104.7 0.0 copy-done.3
  104.7 0.0 copy-done.4
  104.7 0.0 copy-done.6
  104.7 0.0 copy-start.1
  104.7 1.8 copy-done.1
  106.5 151.5 %weight_grad.1 = (f32[56,576]{1,0:T(8,128)S(1)}, f32[8,64]{1,0:T(8,128)S(1)}) custom-call(f32[9,128,576]{2,1,0:T(8,128)S(1)} %bitcast.13, f32[128,576]{1,0:T(8,128)S(1)} %copy-done.4, f32[1,512]{1,0:T(1,128)S(1)} %bitcast.15, f32[128,32]{1,0:T(8,128)S(1)} %copy-done.3, f32[128,32]{1,0:T(8,128)S(1)} %copy-done.2, bf16[128,7168]{1,0:T(8,128)(2,1)S(1)} %bitcast.12, ...), custom_call_target="tpu_custom_call" | custom-call | tf_op jit(solution)/shard_map/weight_grad/pallas_call | solution.py:786
  258.0 0.1 reshape.32
  258.1 0.5 reduce_max.9
  258.6 0.7 copy.10
  (2 shorter events, 0.0 us)
Async XLA Ops:
  2.0 58.5 %copy-start.5 = (f32[128,64]{1,0:T(8,128)S(1)}, f32[128,64]{1,0:T(8,128)}, u32[]{:S(2)}) copy-start(f32[128,64]{1,0:T(8,128)} %fusion.hot) | copy-start | bytes 98308
  60.6 1.4 copy-start.7
  61.9 42.7 %copy-start = (bf16[1,128,7168]{2,1,0:T(8,128)(2,1)S(1)}, bf16[1,128,7168]{2,1,0:T(8,128)(2,1)}, u32[]{:S(2)}) copy-start(bf16[1,128,7168]{2,1,0:T(8,128)(2,1)} %param.6) | copy-start | bytes 5505028
  61.9 42.7 %copy-start.2 = (f32[128,32]{1,0:T(8,128)S(1)}, f32[128,32]{1,0:T(8,128)}, u32[]{:S(2)}) copy-start(f32[128,32]{1,0:T(8,128)} %get-tuple-element.19.sin) | copy-start | bytes 49156
  61.9 42.7 %copy-start.3 = (f32[128,32]{1,0:T(8,128)S(1)}, f32[128,32]{1,0:T(8,128)}, u32[]{:S(2)}) copy-start(f32[128,32]{1,0:T(8,128)} %get-tuple-element.20.cos) | copy-start | bytes 49156
  61.9 42.7 %copy-start.4 = (f32[128,576]{1,0:T(8,128)S(1)}, f32[128,576]{1,0:T(8,128)}, u32[]{:S(2)}) copy-start(f32[128,576]{1,0:T(8,128)} %get-tuple-element.15.proj) | copy-start | bytes 884740
  61.9 42.7 %copy-start.6 = (f32[512]{0:T(512)S(1)}, f32[512]{0:T(512)}, u32[]{:S(2)}) copy-start(f32[512]{0:T(512)} %param.8) | copy-start | bytes 6148
  104.7 1.8 copy-start.1

commit v3 on v2

--- a/solution.py
+++ b/solution.py
@@ -495,32 +495,33 @@
         part[p, :, :KV] = whole[p * PIECE : (p + 1) * PIECE]
         for r in range(8):
             part[p, r : r + 1, KV:] = top[r : r + 1, r * ROPE : (r + 1) * ROPE]
-    halves = []
-    for n in range(CTX // 2):
-        copy = send(part.at[2 * n + 1 - k], part_in.at[n], ss.at[n], sr.at[n], sibling)
-        copy.start()
-        halves.append(copy)
+    me_n = c // 2
+    order = [*range(1, CTX // 2), 0]
+    piece = [(me_n - s + 8) % 8 for s in range(CTX // 2)]
+    halves = {}
+    for s in order:
+        copy = send(part.at[2 * piece[s] + 1 - k], part_in.at[s], ss.at[s], sr.at[s], sibling)
+        copy.start()
+        halves[s] = copy
     totals = []
-    me_n = c // 2
-    for n in range(CTX // 2):
-        halves[n].wait_recv()
-        here = part.at[2 * n + k]
-        sums[n, :, :KV] = here[:, :KV] + part_in[n, :, :KV]
-        sums[n, :8, KV:] = jnp.maximum(here[:8, KV:], part_in[n, :8, KV:])
-    for s in range(1, CTX // 2):
-        to = (me_n - s + 8) % 8
-        copy = send(sums.at[to], sums_in.at[s], ts.at[s], tr.at[s], back[s - 1])
-        copy.start()
-        totals.append(copy)
-    rows = sums[me_n, :, :KV]
-    top = sums[me_n, :8, KV:]
+    for s in order:
+        halves[s].wait_recv()
+        here = part.at[2 * piece[s] + k]
+        sums[s, :, :KV] = here[:, :KV] + part_in[s, :, :KV]
+        sums[s, :8, KV:] = jnp.maximum(here[:8, KV:], part_in[s, :8, KV:])
+        if s > 0:
+            copy = send(sums.at[s], sums_in.at[s], ts.at[s], tr.at[s], back[s - 1])
+            copy.start()
+            totals.append(copy)
+    rows = sums[0, :, :KV]
+    top = sums[0, :8, KV:]
     for s in range(1, CTX // 2):
         totals[s - 1].wait_recv()
         rows = rows + sums_in[s, :, :KV]
         top = jnp.maximum(top, sums_in[s, :8, KV:])
     rows_out[...] = rows
     peak_out[...] = top
-    for copy in swaps + tokens + gathers + sends + spread + halves + totals:
+    for copy in swaps + tokens + gathers + sends + spread + list(halves.values()) + totals:
         copy.wait_send()
 
 

time: 260 us -> 258 us (level)
  no operation moved by 1% of the time
where the time goes in v3:
time: 258 us
  Pallas kernels  250 us (97%)
  local copies, waits for them, and re-layouts  3.95 us (2%)
  other arithmetic  2.88 us (1%)
    pallas_call x1, Pallas kernels, weight_update(): pl.pallas_call(update_kernel, out_shape=(jax.ShapeDtypeStruct((PIECE, KV)...  150 us
    pallas_call x1, Pallas kernels, make_keys(): pl.pallas_call(keys_kernel, out_shape=(jax.ShapeDtypeStruct((SLOTS, BLOCK...  57.5 us
    pallas_call x1, Pallas kernels, attention(): pl.pallas_call(attention_kernel, grid=(TILES,), in_specs=[per_tile(KV), p...  42.7 us

profile of v3, /device:TPU:1, one launch (start us, length us, event | category | flops | bytes accessed | tf_op | source)
XLA Modules:
  0.0 257.7 jit_solution(10302387532103860745)
XLA Ops:
  0.7 1.4 fusion.hot
  2.0 0.0 copy-start.5
  2.0 1.0 multiply_sine_fusion
  3.0 57.5 %keys.1 = (bf16[9,128,640]{2,1,0:T(8,128)(2,1)}, f32[128,576]{1,0:T(8,128)}, bf16[4096,576]{1,0:T(8,128)(2,1)}) custom-call(bf16[128,7168]{1,0:T(8,128)(2,1)} %bitcast.11, bf16[576,896]{1,0:T(8,128)(2,1)} %bitcast.18, f32[1,512]{1,0:T(1,128)} %bitcast.14, f32[128,64]{1,0:T(8,128)} %fusion.hot, f32[128,32]{1,0:T(8,128)} %get-tuple-element.20.cos, ...), custom_call_target="tpu_custom_call" | custom-call | tf_op jit(solution)/shard_map/keys/pallas_call | solution.py:291
  60.6 0.0 copy-done.5
  60.6 0.0 copy-start.7
  60.6 1.4 copy-done.7
  61.9 0.0 copy-start
  61.9 0.0 copy-start.2
  61.9 0.0 copy-start.3
  61.9 0.0 copy-start.4
  61.9 0.0 copy-start.6
  62.0 42.7 %attention.1 = (bf16[4096,512]{1,0:T(8,128)(2,1)}, f32[1152,576]{1,0:T(8,128)}, f32[8,512]{1,0:T(8,128)S(1)}) custom-call(bf16[4096,576]{1,0:T(8,128)(2,1)} %get-tuple-element.11.q, bf16[4096,512]{1,0:T(8,128)(2,1)} %bitcast.20, f32[128,64]{1,0:T(8,128)S(1)} %copy-done.5, bf16[1152,640]{1,0:T(8,128)(2,1)S(1)} %bitcast.16), custom_call_target="tpu_custom_call" | custom-call | flops 12683575296 | bytes 16777216 | tf_op jit(solution)/shard_map/attention/pallas_call | solution.py:371
  104.7 0.0 copy-done
  104.7 0.0 copy-done.2
  104.7 0.0 copy-done.3
  104.7 0.0 copy-done.4
  104.7 0.0 copy-done.6
  104.7 0.0 copy-start.1
  104.7 1.8 copy-done.1
  106.5 149.9 %weight_grad.1 = (f32[56,576]{1,0:T(8,128)S(1)}, f32[8,64]{1,0:T(8,128)S(1)}) custom-call(f32[9,128,576]{2,1,0:T(8,128)S(1)} %bitcast.13, f32[128,576]{1,0:T(8,128)S(1)} %copy-done.4, f32[1,512]{1,0:T(1,128)S(1)} %bitcast.15, f32[128,32]{1,0:T(8,128)S(1)} %copy-done.3, f32[128,32]{1,0:T(8,128)S(1)} %copy-done.2, bf16[128,7168]{1,0:T(8,128)(2,1)S(1)} %bitcast.12, ...), custom_call_target="tpu_custom_call" | custom-call | tf_op jit(solution)/shard_map/weight_grad/pallas_call | solution.py:787
  256.4 0.1 reshape.32
  256.5 0.5 reduce_max.9
  257.0 0.7 copy.10
  (2 shorter events, 0.0 us)
Async XLA Ops:
  2.0 58.5 %copy-start.5 = (f32[128,64]{1,0:T(8,128)S(1)}, f32[128,64]{1,0:T(8,128)}, u32[]{:S(2)}) copy-start(f32[128,64]{1,0:T(8,128)} %fusion.hot) | copy-start | bytes 98308
  60.6 1.4 copy-start.7
  61.9 42.7 %copy-start = (bf16[1,128,7168]{2,1,0:T(8,128)(2,1)S(1)}, bf16[1,128,7168]{2,1,0:T(8,128)(2,1)}, u32[]{:S(2)}) copy-start(bf16[1,128,7168]{2,1,0:T(8,128)(2,1)} %param.6) | copy-start | bytes 5505028
  61.9 42.7 %copy-start.2 = (f32[128,32]{1,0:T(8,128)S(1)}, f32[128,32]{1,0:T(8,128)}, u32[]{:S(2)}) copy-start(f32[128,32]{1,0:T(8,128)} %get-tuple-element.19.sin) | copy-start | bytes 49156
  61.9 42.7 %copy-start.3 = (f32[128,32]{1,0:T(8,128)S(1)}, f32[128,32]{1,0:T(8,128)}, u32[]{:S(2)}) copy-start(f32[128,32]{1,0:T(8,128)} %get-tuple-element.20.cos) | copy-start | bytes 49156
  61.9 42.7 %copy-start.4 = (f32[128,576]{1,0:T(8,128)S(1)}, f32[128,576]{1,0:T(8,128)}, u32[]{:S(2)}) copy-start(f32[128,576]{1,0:T(8,128)} %get-tuple-element.15.proj) | copy-start | bytes 884740
  61.9 42.7 %copy-start.6 = (f32[512]{0:T(512)S(1)}, f32[512]{0:T(512)}, u32[]{:S(2)}) copy-start(f32[512]{0:T(512)} %param.8) | copy-start | bytes 6148
  104.7 1.8 copy-start.1
